TPU v7x, 256 devices: a whole 4x4x8 slice. The times are simulated.
256 devices in a mesh: batch: 32 (over x, z), node: 4 (over y), replica: 2 (over core).
Axes of the slice: x: 4, y: 4, z: 8, core: 2. Of those that a mesh axis runs over, the one named last changes fastest.
Arguments:
- embed_table: bfloat16 [32768, 1024], P('batch'), may hold values from -6 to 6
- owner_shard: int32 [64, 256, 1], P(('batch', 'replica')), may hold values from 0 to 31; in each aligned block of 256 rows (0 to 255, 256 to 511, ..., all dimensions but the last counted through in order) at most 12 rows name the same one
- local_row: int32 [64, 256], P(('batch', 'replica')), may hold values from 0 to 1023
- lengths: int32 [64], P(('batch', 'replica')), may hold values from 64 to 256
- spd_bucket: int32 [64, 256, 256], P(('batch', 'replica')), may hold values from 0 to 15, as said below
- degree_bucket: int32 [64, 256], P(('batch', 'replica')), may hold values from 0 to 31, as said below
- w_query: bfloat16 [1024, 1024], P(None, 'node'), may hold values from -0.1875 to 0.1875
- w_key: bfloat16 [1024, 1024], P(None, 'node'), may hold values from -0.1875 to 0.1875
- w_value: bfloat16 [1024, 1024], P(None, 'node'), may hold values from -0.1875 to 0.1875
- w_out: bfloat16 [1024, 1024], P('node'), may hold values from -0.1875 to 0.1875
- spd_bias: float32 [16, 16], P(None, 'node'), may hold values from -4 to 4
- degree_bias: float32 [32, 16], P(None, 'node'), may hold values from -2 to 253
- cotangent: bfloat16 [64, 256, 1024], P(('batch', 'replica')), may hold values from -6 to 6
Outputs:
- table_grad: float32 [32768, 1024], P('batch', ('node', 'replica'))
- query_grad: float32 [1024, 1024], P(None, 'node')
- key_grad: float32 [1024, 1024], P(None, 'node')
- value_grad: float32 [1024, 1024], P(None, 'node')
- out_grad: float32 [1024, 1024], P('node')
- spd_grad: float32 [16, 16], P(None, 'node')
- degree_grad: float32 [32, 16], P(None, 'node')
Inputs may be any that keep to these rules, and one draw needn't show every extreme that they name: `owner_shard`: in each aligned block of 256 slots (the subgraphs of one index of batch and replica) no owner shard is named by more than 12 slots, a bound that some block reaches. `lengths`: slots at or past a subgraph's length are padding. `spd_bucket`: symmetric in its last two dimensions, 0 exactly on the diagonal. `degree_bucket`: some subgraphs hold only buckets below half of 32.
All inputs are finite; a program needn't handle non-finite values.
Results may differ from a plain program's by a relative error of at most 0.015.
Values may be sent and summed in bfloat16 or wider, within the bound.
A program may use at most 64 MiB of HBM per device.

v0:
```python
import jax
import jax.numpy as jnp
from jax import lax
from jax.sharding import PartitionSpec as P

HEAD_DIM = 64
NSPD = 16
NDEG = 32
EPS = 1e-05


def normalize(rows_in):
    widened = rows_in.astype(jnp.float32)
    mean_val = jnp.mean(widened, axis=-1, keepdims=True)
    centred = widened - mean_val
    inv_std = lax.rsqrt(jnp.mean(centred * centred, axis=-1, keepdims=True) + EPS)
    return (centred * inv_std, inv_std)


def on_device(
    embed_table,
    owner_shard,
    local_row,
    lengths,
    spd_bucket,
    degree_bucket,
    w_query,
    w_key,
    w_value,
    w_out,
    spd_bias,
    degree_bias,
    cotangent,
):
    group_count, slot_count, feature_dim = cotangent.shape
    slot_total = group_count * slot_count
    row_count = embed_table.shape[0]
    peer_count = lax.axis_size("batch")
    capacity = 3 * slot_total // (2 * peer_count)
    dest_shard = owner_shard.reshape(slot_total)
    wanted = local_row.reshape(slot_total)
    bucket_hits = (dest_shard[:, None] == jnp.arange(peer_count, dtype=jnp.int32)[None, :]).astype(
        jnp.int32
    )
    bucket_rank = jnp.sum((jnp.cumsum(bucket_hits, axis=0) - bucket_hits) * bucket_hits, axis=1)
    slot_place = dest_shard * capacity + bucket_rank
    requests = jnp.full((peer_count * capacity,), -1, jnp.int32).at[slot_place].set(wanted)
    asked_rows = lax.all_to_all(
        requests.reshape(peer_count, capacity), "batch", split_axis=0, concat_axis=0, tiled=True
    ).reshape(peer_count * capacity)
    present = asked_rows >= 0
    safe_rows = jnp.where(present, asked_rows, 0)
    target_rows = jnp.where(present, asked_rows, row_count)
    fetched = lax.all_to_all(
        embed_table[safe_rows].reshape(peer_count, capacity, feature_dim),
        "batch",
        split_axis=0,
        concat_axis=0,
        tiled=True,
    )
    slot_rows = fetched.reshape(peer_count * capacity, feature_dim)[slot_place]
    x_hat, inv_std = normalize(slot_rows)
    normed = x_hat.astype(jnp.bfloat16)
    local_width = w_query.shape[1]
    head_local = local_width // HEAD_DIM
    head_shape = (group_count, slot_count, head_local, HEAD_DIM)
    score_scale = HEAD_DIM ** (-0.5)

    def project(weight):
        return jnp.dot(normed, weight, preferred_element_type=jnp.float32).astype(jnp.bfloat16)

    queries = project(w_query).reshape(head_shape)
    key_rows = project(w_key).reshape(head_shape)
    values = project(w_value).reshape(head_shape)
    valid_slot = jnp.arange(slot_count, dtype=jnp.int32)[None, :] < lengths[:, None]
    spd_hot = (spd_bucket[..., None] == jnp.arange(NSPD, dtype=jnp.int32)).astype(jnp.float32)
    degree_hot = (degree_bucket[..., None] == jnp.arange(NDEG, dtype=jnp.int32)).astype(jnp.float32)
    spd_term = jnp.einsum("gijb,bh->ghij", spd_hot, spd_bias, precision=lax.Precision.HIGHEST)
    degree_term = jnp.einsum(
        "gjb,bh->ghj", degree_hot, degree_bias, precision=lax.Precision.HIGHEST
    )[:, :, None, :]
    scores = (
        jnp.einsum("gihd,gjhd->ghij", queries, key_rows, preferred_element_type=jnp.float32)
        * score_scale
        + spd_term
        + degree_term
    )
    scores = jnp.where(valid_slot[:, None, None, :], scores, -jnp.inf)
    row_top = jnp.max(scores, axis=-1, keepdims=True)
    exp_scores = jnp.exp(scores - row_top)
    probs = exp_scores / jnp.sum(exp_scores, axis=-1, keepdims=True)
    probs_b = probs.astype(jnp.bfloat16)
    attended = (
        jnp.einsum("ghij,gjhd->gihd", probs_b, values, preferred_element_type=jnp.float32)
        .astype(jnp.bfloat16)
        .reshape(slot_total, local_width)
    )
    d_masked = jnp.where(valid_slot[:, :, None], cotangent, jnp.zeros_like(cotangent)).reshape(
        slot_total, feature_dim
    )
    d_att = jnp.dot(d_masked, w_out.T, preferred_element_type=jnp.float32).astype(jnp.bfloat16)
    out_part = jnp.dot(attended.T, d_masked, preferred_element_type=jnp.float32)
    d_att_h = d_att.reshape(head_shape)
    d_values = (
        jnp.einsum("ghij,gihd->gjhd", probs_b, d_att_h, preferred_element_type=jnp.float32)
        .astype(jnp.bfloat16)
        .reshape(slot_total, local_width)
    )
    d_probs = jnp.einsum("gihd,gjhd->ghij", d_att_h, values, preferred_element_type=jnp.float32)
    d_scores = probs * (d_probs - jnp.sum(probs * d_probs, axis=-1, keepdims=True))
    spd_part = jnp.einsum("gijb,ghij->bh", spd_hot, d_scores, precision=lax.Precision.HIGHEST)
    degree_part = jnp.einsum("gjb,ghij->bh", degree_hot, d_scores, precision=lax.Precision.HIGHEST)
    d_scores_b = d_scores.astype(jnp.bfloat16)
    d_queries = (
        (
            jnp.einsum("ghij,gjhd->gihd", d_scores_b, key_rows, preferred_element_type=jnp.float32)
            * score_scale
        )
        .astype(jnp.bfloat16)
        .reshape(slot_total, local_width)
    )
    d_keys = (
        (
            jnp.einsum("ghij,gihd->gjhd", d_scores_b, queries, preferred_element_type=jnp.float32)
            * score_scale
        )
        .astype(jnp.bfloat16)
        .reshape(slot_total, local_width)
    )
    query_part = jnp.dot(normed.T, d_queries, preferred_element_type=jnp.float32)
    key_part = jnp.dot(normed.T, d_keys, preferred_element_type=jnp.float32)
    value_part = jnp.dot(normed.T, d_values, preferred_element_type=jnp.float32)
    d_normed = (
        jnp.dot(d_queries, w_query.T, preferred_element_type=jnp.float32)
        + jnp.dot(d_keys, w_key.T, preferred_element_type=jnp.float32)
        + jnp.dot(d_values, w_value.T, preferred_element_type=jnp.float32)
    )
    lead_flag = (lax.axis_index("node") == 0).astype(jnp.float32)
    d_rows = lead_flag * d_masked.astype(jnp.float32) + inv_std * (
        d_normed
        - jnp.mean(d_normed, axis=-1, keepdims=True)
        - x_hat * jnp.mean(d_normed * x_hat, axis=-1, keepdims=True)
    )
    send_back = (
        jnp.zeros((peer_count * capacity, feature_dim), jnp.float32).at[slot_place].set(d_rows)
    )
    returned = (
        lax.all_to_all(
            send_back.reshape(peer_count, capacity, feature_dim).astype(jnp.bfloat16),
            "batch",
            split_axis=0,
            concat_axis=0,
            tiled=True,
        )
        .astype(jnp.float32)
        .reshape(peer_count * capacity, feature_dim)
    )
    accum = (
        jnp.zeros((row_count, feature_dim), jnp.float32).at[target_rows].add(returned, mode="drop")
    )
    table_grad = lax.psum_scatter(
        accum.astype(jnp.bfloat16), ("node", "replica"), scatter_dimension=1, tiled=True
    ).astype(jnp.float32)
    summed = lax.psum(
        (query_part, key_part, value_part, out_part, spd_part, degree_part), ("batch", "replica")
    )
    copies = float(peer_count * lax.axis_size("replica"))
    return (
        table_grad,
        summed[0] / copies,
        summed[1] / copies,
        summed[2] / copies,
        summed[3] / copies,
        summed[4] / copies,
        summed[5] / copies,
    )


def solution(mesh):
    placed = (
        P("batch", None),
        P(("batch", "replica"), None, None),
        P(("batch", "replica"), None),
        P(("batch", "replica")),
        P(("batch", "replica"), None, None),
        P(("batch", "replica"), None),
        P(None, "node"),
        P(None, "node"),
        P(None, "node"),
        P("node", None),
        P(None, "node"),
        P(None, "node"),
        P(("batch", "replica"), None, None),
    )
    return jax.shard_map(
        on_device,
        mesh=mesh,
        in_specs=placed,
        out_specs=(
            P("batch", ("node", "replica")),
            P(None, "node"),
            P(None, "node"),
            P(None, "node"),
            P("node", None),
            P(None, "node"),
            P(None, "node"),
        ),
        check_vma=False,
    )
```

profile of v0, /device:TPU:8, one launch (start us, length us, event | category | flops | bytes accessed | tf_op | source)
XLA Modules:
  0.0 310.1 jit_solution(10417535351380792851)
XLA Ops:
  8.0 0.8 fusion.50
  8.8 0.6 reduce-window.6
  9.4 0.2 slice_reduce_fusion
  9.7 0.8 fusion.49
  10.4 0.7 compare_select_fusion.4
  11.1 1.6 scatter_custom_fusion
  12.8 20.9 %all_to_all.19 = s32[32,1,12]{2,1,0:T(1,128)S(1)} all-to-all(s32[32,1,12]{2,1,0:T(1,128)S(1)} %bitcast.120), channel_id=1, replica_groups=mesh['batch'=32,'node'=4,'replica'=2] {'batch'}, dimensions={0} | all-to-all | bytes 3072 | tf_op jit(solution)/shard_map/all_to_all | solution.py:48
  33.7 0.5 broadcast.245
  34.2 0.7 reduce.17
  34.9 0.1 reshape.325
  35.0 0.6 fusion.53
  35.6 2.1 gather_fusion
  37.7 1.1 reshape.327
  38.9 4.7 %all-to-all-start.1 = ((bf16[32,12,1024]{2,1,0:T(8,128)(2,1)}), bf16[32,12,1024]{2,1,0:T(8,128)(2,1)}, u32[]{:S(2)}, u32[]{:S(2)}) async-start(bf16[32,12,1024]{2,1,0:T(8,128)(2,1)} %reshape.327), calls=%async_computation.1 | async-start | bytes 2097152 | tf_op jit(solution)/shard_map/all_to_all | solution.py:54
  43.6 1.3 fusion.2
  44.9 1.4 copy.39
  47.0 0.2 convolution_bitcast_fusion
  47.2 2.3 convolution_convert_fusion.3
  49.5 21.5 %all-to-all-done.1 = bf16[32,12,1024]{2,1,0:T(8,128)(2,1)} async-done(((bf16[32,12,1024]{2,1,0:T(8,128)(2,1)}), bf16[32,12,1024]{2,1,0:T(8,128)(2,1)}, u32[]{:S(2)}, u32[]{:S(2)}) %all-to-all-start.1) | async-done | bytes 786464 | tf_op jit(solution)/shard_map/all_to_all | solution.py:54
  71.1 1.3 reshape.328
  72.4 1.2 gather_fusion.1
  73.6 0.1 convert_reduce_fusion
  73.7 0.3 fusion.26
  74.0 1.5 convolution_convert_fusion.5
  75.5 0.5 convolution_convert_fusion.4
  76.0 0.4 fusion.11
  76.4 0.8 fusion.67
  77.2 0.5 convolution_convert_fusion.2
  77.7 0.4 multiply_reduce_fusion
  78.1 0.2 fusion.66
  78.3 0.2 fusion.17
  78.5 0.8 copy-done.1
  79.3 0.3 fusion.18
  79.5 1.9 convolution_convert_fusion.1
  81.5 2.4 fusion.68
  83.9 1.4 fusion.60
  85.3 1.9 convolution_convert_fusion
  87.3 1.5 fusion.58
  88.7 1.5 fusion.56
  90.2 1.4 fusion.31
  91.6 0.2 reduce-scatter.4.cloned.1.call-start
  91.8 1.8 convolution_add_fusion.1
  93.6 1.4 fusion.65
  95.0 3.8 %scatter_custom_fusion.1 = f32[384,1024]{1,0:T(8,128)} fusion(s32[256]{0:T(256)} %bitcast.125, bf16[256,1024]{1,0:T(8,128)(2,1)S(1)} %gather_fusion.1, f32[256,1024]{1,0:T(8,128)} %get-tuple-element.23, f32[]{:T(128)} %constant.15.clone.1, f32[256]{0:T(256)S(1)} %get-tuple-element.24, f32[256]{0:T(256)S(1)} %get-tuple-element.25, ...), kind=kCustom, calls=%fused_computation.44 | custom fusion | flops 2883584 | bytes 3674884 | tf_op jit(solution)/shard_map/scatter | solution.py:145
  98.8 2.5 convert_element_type.111
  101.3 1.2 convert_element_type.112
  102.5 35.3 %all_to_all.20 = bf16[32,12,1024]{2,1,0:T(8,128)(2,1)} all-to-all(bf16[32,12,1024]{2,1,0:T(8,128)(2,1)S(1)} %convert_element_type.112), channel_id=1, replica_groups=mesh['batch'=32,'node'=4,'replica'=2] {'batch'}, dimensions={0} | all-to-all | bytes 1572864 | tf_op jit(solution)/shard_map/all_to_all | solution.py:148
  137.9 2.4 reshape.377
  140.2 6.6 %scatter_custom_fusion.2 = f32[1024,1024]{1,0:T(8,128)} fusion(s32[384]{0:T(512)} %get-tuple-element.10, f32[384,1024]{1,0:T(8,128)} %reshape.377, f32[]{:T(128)} %constant.15.clone.1), kind=kCustom, calls=%fused_computation.11 | custom fusion | flops 393216 | bytes 4194816 | tf_op jit(solution)/shard_map/scatter-add | solution.py:159
  146.9 3.9 %convert_element_type.113 = bf16[1024,1024]{1,0:T(8,128)(2,1)} convert(f32[1024,1024]{1,0:T(8,128)} %scatter_custom_fusion.2) | non-fusion elementwise | flops 1048576 | bytes 6291456 | tf_op jit(solution)/shard_map/convert_element_type | solution.py:162
  150.8 4.0 %copy.52 = bf16[1024,1024]{0,1:T(8,128)(2,1)} copy(bf16[1024,1024]{1,0:T(8,128)(2,1)} %convert_element_type.113) | data formatting | bytes 4194304
  154.8 1.2 copy-done.2
  156.0 1.3 copy.46
  157.3 4.0 %fusion.19 = f32[16,4]{0,1:T(4,128)S(1)} fusion(f32[4,256,256]{2,0,1:T(4,128)} %copy.46, s32[256,256]{1,0:T(8,128)S(1)} %bitcast.117), kind=kOutput, calls=%fused_computation.39 | convolution fusion | flops 51380224 | bytes 1310976 | tf_op jit(solution)/shard_map/gijb,ghij->bh/dot_general | solution.py:111
  161.2 0.2 fusion.44
  161.5 127.4 %all-reduce = (f32[16,4]{0,1:T(4,128)S(1)}, f32[32,4]{0,1:T(4,128)S(1)}) all-reduce(f32[16,4]{0,1:T(4,128)S(1)} %fusion.19, f32[32,4]{0,1:T(4,128)S(1)} %fusion.44), channel_id=1, replica_groups=mesh['batch'=32,'node'=4,'replica'=2] {'batch','replica'}, use_global_device_ids=true, to_apply=%region_18.19 | all-reduce | flops 192 | bytes 1536 | tf_op jit(solution)/shard_map/psum | solution.py:164
  288.9 0.6 broadcast_multiply_fusion.5
  289.5 0.6 broadcast_multiply_fusion.4
  290.0 5.7 %all-reduce.4.cloned.1.call-done = (f32[1024,256]{1,0:T(8,128)}, f32[1024,256]{1,0:T(8,128)}, f32[1024,256]{1,0:T(8,128)}, f32[256,1024]{1,0:T(8,128)}) async-done(((f32[1024,256]{1,0:T(8,128)}, f32[1024,256]{1,0:T(8,128)}, f32[1024,256]{1,0:T(8,128)}, f32[256,1024]{1,0:T(8,128)}), (f32[1024,256]{1,0:T(8,128)}, f32[1024,256]{1,0:T(8,128)}, f32[1024,256]{1,0:T(8,128)}, ...) | async-done | bytes 4194320 | tf_op jit(solution)/shard_map/psum | solution.py:164
  295.7 2.4 broadcast_multiply_fusion.3
  298.1 1.1 broadcast_multiply_fusion
  299.2 1.5 broadcast_multiply_fusion.1
  300.7 1.1 copy.53
  301.8 0.8 convert_element_type.114
  (51 shorter events, 0.4 us)
Async XLA Ops:
  8.0 27.6 %copy-start = (bf16[1024,1024]{1,0:T(8,128)(2,1)S(1)}, bf16[1024,1024]{1,0:T(8,128)(2,1)}, u32[]{:S(2)}) copy-start(bf16[1024,1024]{1,0:T(8,128)(2,1)} %param.13) | copy-start | bytes 6291460
  11.1 35.8 %copy-start.14 = (s32[256,1]{0,1:T(1,128)}, s32[256,1]{0,1:T(1,128)S(1)}, u32[]{:S(2)}) copy-start(s32[256,1]{0,1:T(1,128)S(1)} %compare_select_fusion.4) | copy-start | bytes 3076
  37.7 5.9 %copy-start.12 = (s32[1,256,256]{2,1,0:T(8,128)S(1)}, s32[1,256,256]{2,1,0:T(8,128)}, u32[]{:S(2)}) copy-start(s32[1,256,256]{2,1,0:T(8,128)} %param.17) | copy-start | bytes 786436
  37.7 5.9 %copy-start.15 = (f32[16,4]{0,1:T(4,128)S(1)}, f32[16,4]{0,1:T(4,128)}, u32[]{:S(2)}) copy-start(f32[16,4]{0,1:T(4,128)} %param.23) | copy-start | bytes 772
  38.9 32.2 %all-to-all-start.1 = ((bf16[32,12,1024]{2,1,0:T(8,128)(2,1)}), bf16[32,12,1024]{2,1,0:T(8,128)(2,1)}, u32[]{:S(2)}, u32[]{:S(2)}) async-start(bf16[32,12,1024]{2,1,0:T(8,128)(2,1)} %reshape.327), calls=%async_computation.1 | async-start | bytes 2097152 | tf_op jit(solution)/shard_map/all_to_all | solution.py:54
  43.5 3.4 %copy-start.16 = (f32[32,4]{0,1:T(4,128)S(1)}, f32[32,4]{0,1:T(4,128)}, u32[]{:S(2)}) copy-start(f32[32,4]{0,1:T(4,128)} %param.24) | copy-start | bytes 1540
  43.5 3.4 %copy-start.17 = (s32[1,256]{1,0:T(1,128)S(1)}, s32[1,256]{1,0:T(1,128)}, u32[]{:S(2)}) copy-start(s32[1,256]{1,0:T(1,128)} %param.18) | copy-start | bytes 3076
  43.5 252.2 %all-reduce.4.cloned.1.call-start = ((), (), s32[]{:S(2)}) async-start(), calls=%async_computation.5 | async-start | bytes 8388608 | tf_op jit(solution)/shard_map/psum | solution.py:164
  73.6 2.0 copy-start.11
  73.6 2.4 copy-start.3
  76.0 1.2 copy-start.9
  76.4 1.6 copy-start.4
  76.4 1.3 copy-start.19
  78.3 1.0 copy-start.1
  87.3 2.9 copy-start.5
  91.6 209.1 %reduce-scatter.4.cloned.1.call-start = ((), (), s32[]{:S(2)}) async-start(), calls=%async_computation.4 | async-start | bytes 2359296
  91.8 1.8 copy-start.10
  154.7 1.2 copy-start.2
  154.7 2.5 copy-start.13
  156.0 5.3 %copy-start.18 = (s32[1,256]{1,0:T(1,128)S(1)}, s32[1,256]{1,0:T(1,128)}, u32[]{:S(2)}) copy-start(s32[1,256]{1,0:T(1,128)} %param.18) | copy-start | bytes 3076
  295.7 2.4 copy-start.6
  295.7 3.5 %copy-start.7 = (f32[1024,256]{1,0:T(8,128)S(1)}, f32[1024,256]{1,0:T(8,128)}, u32[]{:S(2)}) copy-start(f32[1024,256]{1,0:T(8,128)} %get-tuple-element.14) | copy-start | bytes 3145732
  295.7 3.5 %copy-start.8 = (f32[1024,256]{1,0:T(8,128)S(1)}, f32[1024,256]{1,0:T(8,128)}, u32[]{:S(2)}) copy-start(f32[1024,256]{1,0:T(8,128)} %get-tuple-element.15) | copy-start | bytes 3145732
Sparse Core Ops, SparseCore 0:
  91.7 203.9 all-reduce.3
Sparse Core Ops, SparseCore 1:
  154.8 32.6 reduce-scatter.3
where the time goes:
time: 311 us; the launch traced here: 310 us
  blocking collectives  184 us (59%)
  other arithmetic  29.4 us (9%)
  waiting for transfers between devices  27.2 us (9%)
  matrix products  26.8 us (9%)
  local copies, waits for them, and re-layouts  21.6 us (7%)
  between operations  16.5 us (5%)
  starting transfers between devices  4.93 us (2%)
    psum x1, blocking collectives, on_device(): lax.psum((query_part, key_part, value_part, out_part, spd_part, degree_pa...  127 us
    all_to_all x1, blocking collectives, on_device(): lax.all_to_all(send_back.reshape(peer_count, capacity, feature_dim).astyp...  35.3 us
    all_to_all x1, waiting for transfers between devices, on_device(): lax.all_to_all(embed_table[safe_rows].reshape(peer_count, capacity, featu...  21.5 us
    all_to_all x1, blocking collectives, on_device(): lax.all_to_all(requests.reshape(peer_count, capacity), 'batch', split_axi...  20.9 us
    unnamed x42, local copies, waits for them, and re-layouts  7.15 us
    scatter-add x1, other arithmetic, on_device(): jnp.zeros((row_count, feature_dim), jnp.float32).at[target_rows]  6.64 us
  transfers between devices with their start and end apart: 3, of which 2 were waited for; matrix products, arithmetic and copies ran while one was open for 14% of the time, Pallas kernels for 0%

commit v1 on v0

--- a/solution.py
+++ b/solution.py
@@ -162,7 +162,8 @@
         accum.astype(jnp.bfloat16), ("node", "replica"), scatter_dimension=1, tiled=True
     ).astype(jnp.float32)
     summed = lax.psum(
-        (query_part, key_part, value_part, out_part, spd_part, degree_part), ("batch", "replica")
+        lax.psum((query_part, key_part, value_part, out_part, spd_part, degree_part), "replica"),
+        "batch",
     )
     copies = float(peer_count * lax.axis_size("replica"))
     return (

time: 311 us -> 332 us (1.068)
  waiting for transfers between devices: 27.2 us -> 105 us
  blocking collectives: 184 us -> 128 us
    psum x1, blocking collectives: 127 us -> 2.46 us  [on_device(): lax.psum((query_part, key_part, value_part, out_part, spd_part, degree_pa...]
    psum x0 -> x1, waiting for transfers between devices: none -> 82.3 us  [on_device(): lax.psum(lax.psum((query_part, key_part, value_part, out_part, spd_part,...]
    psum x0 -> x1, blocking collectives: none -> 72.1 us  [on_device(): lax.psum(lax.psum((query_part, key_part, value_part, out_part, spd_part,...]
    psum x1, waiting for transfers between devices: 5.65 us -> 0.02 us  [on_device(): lax.psum((query_part, key_part, value_part, out_part, spd_part, degree_pa...]
    unnamed x42 -> x48, local copies, waits for them, and re-layouts: 7.15 us -> 6.51 us
  transfers between devices with their start and end apart: 3 -> 4, of which waited for: 2 -> 2; matrix products, arithmetic and copies ran while one was open for 14% -> 13% of each run, Pallas kernels for 0% -> 0%
where the time goes in v1:
time: 332 us; the launch traced here: 331 us
  blocking collectives  128 us (39%)
  waiting for transfers between devices  105 us (32%)
  other arithmetic  29.3 us (9%)
  matrix products  26.5 us (8%)
  local copies, waits for them, and re-layouts  21.1 us (6%)
  between operations  16.5 us (5%)
  starting transfers between devices  4.97 us (1%)
    psum x1, waiting for transfers between devices, on_device(): lax.psum(lax.psum((query_part, key_part, value_part, out_part, spd_part,...  82.3 us
    psum x1, blocking collectives, on_device(): lax.psum(lax.psum((query_part, key_part, value_part, out_part, spd_part,...  72.1 us
    all_to_all x1, blocking collectives, on_device(): lax.all_to_all(send_back.reshape(peer_count, capacity, feature_dim).astyp...  32.3 us
    all_to_all x1, waiting for transfers between devices, on_device(): lax.all_to_all(embed_table[safe_rows].reshape(peer_count, capacity, featu...  21.6 us
    all_to_all x1, blocking collectives, on_device(): lax.all_to_all(requests.reshape(peer_count, capacity), 'batch', split_axi...  20.9 us
    scatter-add x1, other arithmetic, on_device(): jnp.zeros((row_count, feature_dim), jnp.float32).at[target_rows]  6.64 us
  transfers between devices with their start and end apart: 4, of which 2 were waited for; matrix products, arithmetic and copies ran while one was open for 13% of the time, Pallas kernels for 0%

profile of v1, /device:TPU:8, one launch (start us, length us, event | category | flops | bytes accessed | tf_op | source)
XLA Modules:
  0.0 330.8 jit_solution(12936966542751065852)
XLA Ops:
  8.0 0.8 fusion.50
  8.8 0.6 reduce-window.6
  9.4 0.2 slice_reduce_fusion
  9.7 0.8 fusion.49
  10.4 0.7 compare_select_fusion.4
  11.1 1.6 scatter_custom_fusion
  12.8 20.9 %all_to_all.19 = s32[32,1,12]{2,1,0:T(1,128)S(1)} all-to-all(s32[32,1,12]{2,1,0:T(1,128)S(1)} %bitcast.120), channel_id=1, replica_groups=mesh['batch'=32,'node'=4,'replica'=2] {'batch'}, dimensions={0} | all-to-all | bytes 3072 | tf_op jit(solution)/shard_map/all_to_all | solution.py:48
  33.7 0.5 broadcast.245
  34.2 0.7 reduce.17
  35.0 0.6 fusion.53
  35.6 2.1 gather_fusion
  37.7 1.1 reshape.327
  38.9 4.7 %all-to-all-start.1 = ((bf16[32,12,1024]{2,1,0:T(8,128)(2,1)}), bf16[32,12,1024]{2,1,0:T(8,128)(2,1)}, u32[]{:S(2)}, u32[]{:S(2)}) async-start(bf16[32,12,1024]{2,1,0:T(8,128)(2,1)} %reshape.327), calls=%async_computation.1 | async-start | bytes 2097152 | tf_op jit(solution)/shard_map/all_to_all | solution.py:54
  43.6 1.3 fusion.2
  44.9 1.4 copy.39
  47.0 0.2 convolution_bitcast_fusion
  47.2 2.3 convolution_convert_fusion.3
  49.5 21.6 %all-to-all-done.1 = bf16[32,12,1024]{2,1,0:T(8,128)(2,1)} async-done(((bf16[32,12,1024]{2,1,0:T(8,128)(2,1)}), bf16[32,12,1024]{2,1,0:T(8,128)(2,1)}, u32[]{:S(2)}, u32[]{:S(2)}) %all-to-all-start.1) | async-done | bytes 786464 | tf_op jit(solution)/shard_map/all_to_all | solution.py:54
  71.1 1.3 reshape.328
  72.4 1.2 gather_fusion.1
  73.7 0.3 fusion.26
  74.0 1.5 convolution_convert_fusion.5
  75.5 0.5 convolution_convert_fusion.4
  76.0 0.4 fusion.11
  76.4 0.8 fusion.67
  77.2 0.5 convolution_convert_fusion.2
  77.7 0.4 multiply_reduce_fusion
  78.1 0.2 fusion.66
  78.3 0.2 fusion.17
  78.5 0.8 copy-done.1
  79.3 0.3 fusion.18
  79.6 2.1 convolution_convert_fusion.1
  81.7 2.8 convolution_convert_fusion
  84.5 1.4 fusion.60
  85.9 1.5 fusion.58
  87.4 1.4 fusion.56
  88.8 1.3 fusion.31
  90.2 0.2 reduce-scatter.4.cloned.1.call-start
  90.5 1.4 fusion.68
  91.9 1.4 convolution_add_fusion.1
  93.3 1.4 fusion.65
  94.8 3.8 %scatter_custom_fusion.1 = f32[384,1024]{1,0:T(8,128)} fusion(s32[256]{0:T(256)} %bitcast.125, bf16[256,1024]{1,0:T(8,128)(2,1)S(1)} %gather_fusion.1, f32[256,1024]{1,0:T(8,128)} %get-tuple-element.29, f32[]{:T(128)} %constant.15.clone.1, f32[256]{0:T(256)S(1)} %get-tuple-element.30, f32[256]{0:T(256)S(1)} %get-tuple-element.31, ...), kind=kCustom, calls=%fused_computation.44 | custom fusion | flops 2883584 | bytes 3674884 | tf_op jit(solution)/shard_map/scatter | solution.py:145
  98.5 2.4 convert_element_type.111
  101.0 1.4 convert_element_type.112
  102.4 32.3 %all_to_all.20 = bf16[32,12,1024]{2,1,0:T(8,128)(2,1)} all-to-all(bf16[32,12,1024]{2,1,0:T(8,128)(2,1)S(1)} %convert_element_type.112), channel_id=1, replica_groups=mesh['batch'=32,'node'=4,'replica'=2] {'batch'}, dimensions={0} | all-to-all | bytes 1572864 | tf_op jit(solution)/shard_map/all_to_all | solution.py:148
  134.7 2.4 reshape.377
  137.1 6.6 %scatter_custom_fusion.2 = f32[1024,1024]{1,0:T(8,128)} fusion(s32[384]{0:T(512)} %get-tuple-element.10, f32[384,1024]{1,0:T(8,128)} %reshape.377, f32[]{:T(128)} %constant.15.clone.1), kind=kCustom, calls=%fused_computation.11 | custom fusion | flops 393216 | bytes 4194816 | tf_op jit(solution)/shard_map/scatter-add | solution.py:159
  143.7 3.8 %convert_element_type.113 = bf16[1024,1024]{1,0:T(8,128)(2,1)} convert(f32[1024,1024]{1,0:T(8,128)} %scatter_custom_fusion.2) | non-fusion elementwise | flops 1048576 | bytes 6291456 | tf_op jit(solution)/shard_map/convert_element_type | solution.py:162
  147.6 4.0 %copy.52 = bf16[1024,1024]{0,1:T(8,128)(2,1)} copy(bf16[1024,1024]{1,0:T(8,128)(2,1)} %convert_element_type.113) | data formatting | bytes 4194304
  151.6 0.7 all-reduce.7.cloned.1.call-update
  152.3 0.5 copy-done.2
  152.9 1.3 copy.46
  154.2 3.9 %fusion.19 = f32[16,4]{0,1:T(4,128)S(1)} fusion(f32[4,256,256]{2,0,1:T(4,128)} %copy.46, s32[256,256]{1,0:T(8,128)S(1)} %bitcast.117), kind=kOutput, calls=%fused_computation.39 | convolution fusion | flops 51380224 | bytes 1310976 | tf_op jit(solution)/shard_map/gijb,ghij->bh/dot_general | solution.py:111
  158.1 0.2 fusion.44
  158.4 2.5 all-reduce.2
  160.8 72.1 %all-reduce = (f32[16,4]{0,1:T(4,128)S(1)}, f32[32,4]{0,1:T(4,128)S(1)}) all-reduce(f32[16,4]{0,1:T(4,128)S(1)} %get-tuple-element.17, f32[32,4]{0,1:T(4,128)S(1)} %get-tuple-element.18), channel_id=1, replica_groups=mesh['batch'=32,'node'=4,'replica'=2] {'batch'}, use_global_device_ids=true, to_apply=%region_23.24 | all-reduce | flops 192 | bytes 1536 | tf_op jit(solution)/shard_map/psum | solution.py:164
  232.9 0.6 broadcast_multiply_fusion.5
  233.5 0.6 broadcast_multiply_fusion.4
  234.1 1.1 copy.53
  235.2 0.8 convert_element_type.114
  236.1 82.3 %all-reduce.7.cloned.1.call-done = (f32[1024,256]{1,0:T(8,128)}, f32[1024,256]{1,0:T(8,128)}, f32[1024,256]{1,0:T(8,128)}, f32[256,1024]{1,0:T(8,128)}) async-done(((f32[1024,256]{1,0:T(8,128)}, f32[1024,256]{1,0:T(8,128)}, f32[1024,256]{1,0:T(8,128)}, f32[256,1024]{1,0:T(8,128)}), (f32[1024,256]{1,0:T(8,128)}, f32[1024,256]{1,0:T(8,128)}, f32[1024,256]{1,0:T(8,128)}, ...) | async-done | bytes 4194320 | tf_op jit(solution)/shard_map/psum | solution.py:164
  318.4 2.4 broadcast_multiply_fusion.3
  320.8 1.1 broadcast_multiply_fusion
  321.9 1.5 broadcast_multiply_fusion.1
  (61 shorter events, 0.7 us)
Async XLA Ops:
  8.0 27.6 %copy-start = (bf16[1024,1024]{1,0:T(8,128)(2,1)S(1)}, bf16[1024,1024]{1,0:T(8,128)(2,1)}, u32[]{:S(2)}) copy-start(bf16[1024,1024]{1,0:T(8,128)(2,1)} %param.13) | copy-start | bytes 6291460
  11.1 35.8 %copy-start.15 = (s32[256,1]{0,1:T(1,128)}, s32[256,1]{0,1:T(1,128)S(1)}, u32[]{:S(2)}) copy-start(s32[256,1]{0,1:T(1,128)S(1)} %compare_select_fusion.4) | copy-start | bytes 3076
  37.7 5.9 %copy-start.12 = (s32[1,256,256]{2,1,0:T(8,128)S(1)}, s32[1,256,256]{2,1,0:T(8,128)}, u32[]{:S(2)}) copy-start(s32[1,256,256]{2,1,0:T(8,128)} %param.17) | copy-start | bytes 786436
  37.7 5.9 %copy-start.16 = (f32[16,4]{0,1:T(4,128)S(1)}, f32[16,4]{0,1:T(4,128)}, u32[]{:S(2)}) copy-start(f32[16,4]{0,1:T(4,128)} %param.23) | copy-start | bytes 772
  38.9 32.2 %all-to-all-start.1 = ((bf16[32,12,1024]{2,1,0:T(8,128)(2,1)}), bf16[32,12,1024]{2,1,0:T(8,128)(2,1)}, u32[]{:S(2)}, u32[]{:S(2)}) async-start(bf16[32,12,1024]{2,1,0:T(8,128)(2,1)} %reshape.327), calls=%async_computation.1 | async-start | bytes 2097152 | tf_op jit(solution)/shard_map/all_to_all | solution.py:54
  43.5 3.4 %copy-start.17 = (f32[32,4]{0,1:T(4,128)S(1)}, f32[32,4]{0,1:T(4,128)}, u32[]{:S(2)}) copy-start(f32[32,4]{0,1:T(4,128)} %param.24) | copy-start | bytes 1540
  43.5 3.4 %copy-start.18 = (s32[1,256]{1,0:T(1,128)S(1)}, s32[1,256]{1,0:T(1,128)}, u32[]{:S(2)}) copy-start(s32[1,256]{1,0:T(1,128)} %param.18) | copy-start | bytes 3076
  43.5 108.1 %all-reduce.9.cloned.1.call-start = ((), (), s32[]{:S(2)}) async-start(), calls=%async_computation.6 | async-start | bytes 8388608 | tf_op jit(solution)/shard_map/psum | solution.py:165
  73.6 2.0 copy-start.11
  73.6 2.4 copy-start.3
  76.0 1.2 copy-start.9
  76.4 1.6 copy-start.4
  76.4 1.3 copy-start.20
  77.7 0.7 copy-start.21
  78.3 1.0 copy-start.1
  79.6 2.1 copy-start.22
  85.9 2.9 copy-start.5
  85.9 2.9 copy-start.14
  90.2 143.9 %reduce-scatter.4.cloned.1.call-start = ((), (), s32[]{:S(2)}) async-start(), calls=%async_computation.4 | async-start | bytes 2359296
  90.5 2.9 copy-start.10
  151.6 166.8 %all-reduce.7.cloned.1.call-start = ((), (), s32[]{:S(2)}) async-start(), calls=%async_computation.5 | async-start | bytes 8388608 | tf_op jit(solution)/shard_map/psum | solution.py:164
  151.6 1.2 copy-start.2
  152.9 1.3 copy-start.13
  152.9 5.3 %copy-start.19 = (s32[1,256]{1,0:T(1,128)S(1)}, s32[1,256]{1,0:T(1,128)}, u32[]{:S(2)}) copy-start(s32[1,256]{1,0:T(1,128)} %param.18) | copy-start | bytes 3076
  318.4 2.4 copy-start.6
  318.4 3.5 %copy-start.7 = (f32[1024,256]{1,0:T(8,128)S(1)}, f32[1024,256]{1,0:T(8,128)}, u32[]{:S(2)}) copy-start(f32[1024,256]{1,0:T(8,128)} %get-tuple-element.14) | copy-start | bytes 3145732
  318.4 3.5 %copy-start.8 = (f32[1024,256]{1,0:T(8,128)S(1)}, f32[1024,256]{1,0:T(8,128)}, u32[]{:S(2)}) copy-start(f32[1024,256]{1,0:T(8,128)} %get-tuple-element.15) | copy-start | bytes 3145732
Sparse Core Ops, SparseCore 0:
  90.3 36.0 all-reduce.8
  156.9 161.4 all-reduce.6
Sparse Core Ops, SparseCore 1:
  151.6 29.6 reduce-scatter.3
